TPU v7x, 128 devices: a whole 4x4x4 slice. The times are simulated.
128 devices in a mesh: src: 16 (over x, z), tgt: 8 (over y, core).
Axes of the slice: x: 4, y: 4, z: 4, core: 2. Of those that a mesh axis runs over, the one named last changes fastest.
Arguments:
- source_embed: bfloat16 [32, 131072], P('tgt', 'src'), may hold values from -4 to 4
- target_embed: bfloat16 [32, 131072], P('src', 'tgt'), may hold values from -4 to 4
- target_potential: float32 [131072], P('tgt'), may hold values from -15 to 15
- log_source_mass: float32 [131072], P('src'), may hold values from -14 to -10
- log_target_mass: float32 [131072], P('tgt'), may hold values from -14 to -10
- tile_list: int32 [16, 8, 2, 64], P('src', 'tgt'), may hold values from 0 to 31, as said below
- counts: int32 [16, 8], P('src', 'tgt'), may hold values from 8 to 64, as said below
Outputs:
- row_potential: float32 [131072], P('src')
- column_potential: float32 [131072], P('tgt')
Inputs may be any that keep to these rules, and one draw needn't show every extreme that they name: `tile_list`: on device (s, t) the first counts[s, t] entries are distinct pairs; every source tile and every target tile lies in some live pair; entries past the count are valid tile numbers but not live. `counts`: some device's count is 64 in every draw.
All inputs are finite; a program needn't handle non-finite values.
Results may differ from a plain program's by a relative error of at most 0.0029.
Values may be sent and summed in bfloat16 or wider, within the bound.
No kernel may reach another device: no remote copies, remote signals or barrier semaphores. Data moves between devices by JAX's collectives and lax.ppermute only.
A program may use at most 64 MiB of HBM per device.

v0:
```python
import functools

import jax
import jax.numpy as jnp
from jax import lax
from jax.experimental import pallas as pl
from jax.experimental.pallas import tpu as pltpu
from jax.sharding import PartitionSpec as P

TILE = 512
LINES = TILE // 128
WIDTH = 32
PIECES = 3
LEFT = 128
RIGHT = 112
DEPTH = 48
TOGETHER = 32
UNROLL = 8
STORES = 4
EPSILON = 0.1
KAPPA = 1.4426950408889634 / EPSILON
ALPHA = KAPPA / WIDTH
GAMMA = KAPPA / (2 * WIDTH)
LOWEST = -1e30
ABSENT = -1.0
TRUSTED = 2.0**-90

BF16, F32 = jnp.bfloat16, jnp.float32
VMEM = pl.BlockSpec(memory_space=pltpu.VMEM)
SMEM = pl.BlockSpec(memory_space=pltpu.SMEM)
HBM = pl.BlockSpec(memory_space=pltpu.HBM)


def in_hbm(value):
    return pltpu.with_memory_space_constraint(value, pltpu.HBM)


def at_tile(tile):
    return pl.ds(pl.multiple_of(tile * TILE, TILE), TILE)


def write_line(ref, tile, line):
    for part in range(LINES):
        ref[pl.ds(tile * LINES + part, 1), :] = line[:, part * 128 : (part + 1) * 128]


def read_line(ref, tile):
    return jnp.concatenate([ref[pl.ds(tile * LINES + part, 1), :] for part in range(LINES)], axis=1)


def highest_of(ref):
    return jnp.max(jnp.max(ref[...], axis=0, keepdims=True), axis=1, keepdims=True)


def pieces(value, number=PIECES):
    terms = []
    for _ in range(number):
        terms.append(value.astype(BF16).astype(F32))
        value = value - terms[-1]
    return terms


def squares(cells):
    return jnp.sum(cells * cells, axis=0, keepdims=True)


def general_lse(red_row, keep_row, list_ref, live, read_red, read_keep, read_bias, out_ref, top, total):
    keep_tiles = top.shape[1] // TILE
    half, scale = float(WIDTH), ALPHA
    rows_of = 64

    def clear(tile, _):
        at = at_tile(tile)
        top[:, at] = jnp.full((8, TILE), LOWEST, F32)
        total[:, at] = jnp.zeros((8, TILE), F32)
        return 0

    def step(entry, _):
        red_tile, keep_tile = list_ref[red_row, entry], list_ref[keep_row, entry]
        keep_at = at_tile(keep_tile)
        cells = read_red(red_tile)
        terms = pieces(half * read_bias(red_tile) - 0.5 * squares(cells))
        filler = jnp.zeros((DEPTH - WIDTH - PIECES, TILE), F32)
        left = jnp.transpose(jnp.concatenate([cells] + terms + [filler, jnp.zeros((LEFT - DEPTH, TILE), F32)], axis=0))
        left = left.astype(BF16)[:, :DEPTH]
        right = jnp.concatenate([read_keep(keep_tile), jnp.ones((PIECES, TILE), F32), filler], axis=0).astype(BF16)
        highest, summed = top[:, keep_at], total[:, keep_at]
        for row in range(0, TILE, rows_of):
            z = jnp.dot(left[row : row + rows_of], right, preferred_element_type=F32)
            z = z.reshape(rows_of // 8, 8, TILE) * scale
            higher = jnp.maximum(highest, jnp.max(z, axis=0))
            summed = summed * jnp.exp2(highest - higher) + jnp.sum(jnp.exp2(z - higher[None]), axis=0)
            highest = higher
        top[:, keep_at] = highest
        total[:, keep_at] = summed
        return 0

    def finish(tile, _):
        at = at_tile(tile)
        highest = jnp.max(top[:, at], axis=0, keepdims=True)
        summed = jnp.sum(total[:, at] * jnp.exp2(top[:, at] - highest), axis=0, keepdims=True)
        value = highest * (1.0 / KAPPA) + EPSILON * jnp.log(jnp.maximum(summed, 1.0))
        write_line(out_ref, tile, value - squares(read_keep(tile)) * (0.5 / WIDTH))
        return 0

    lax.fori_loop(0, keep_tiles, clear, 0)
    lax.fori_loop(0, live, step, 0)
    lax.fori_loop(0, keep_tiles, finish, 0)


def copies_kernel(part_ref, copies_ref):
    for copy in range(copies_ref.shape[0]):
        copies_ref[copy] = part_ref[...]


def source_rows(cells):
    rows = pieces(cells * ALPHA) + [jnp.ones((PIECES, TILE), F32)] + pieces(squares(cells) * -GAMMA)
    rows.append(jnp.zeros((LEFT - PIECES * WIDTH - 2 * PIECES, TILE), F32))
    return jnp.transpose(jnp.concatenate(rows, axis=0)).astype(BF16)


def groups(live, body):
    def one(group, _):
        for member in range(TOGETHER):
            entry = group * TOGETHER + member
            body(entry, member % STORES, entry // STORES)
        return 0

    lax.fori_loop(0, (live + TOGETHER - 1) // TOGETHER, one, 0)


def to_potentials(ref, highest):
    summed = ref[...]
    present = summed >= 0
    value = highest + EPSILON * jnp.log(jnp.maximum(summed, TRUSTED))
    ref[...] = jnp.where(present, value, LOWEST)
    return jnp.min(jnp.where(present, summed, 1.0))


def clear_marks(marks):
    for tile in range(marks.shape[0]):
        marks[tile] = 0


def row_kernel(
    list_hbm, count_ref, source_ref, target_ref, potential_hbm,
    out_ref, source_hbm, target_hbm, store_0, store_1, store_2, store_3,
    left_ref, right, weight, sums, covered, top, total, list_ref, potential_ref, semaphores,
):
    stores = (store_0, store_1, store_2, store_3)
    source_tiles = left_ref.shape[0] // TILE
    target_tiles = right.shape[1] // TILE
    live = count_ref[0, 0]
    rows_of = 64
    fetched = [
        pltpu.make_async_copy(potential_hbm, potential_ref, semaphores.at[2]),
        pltpu.make_async_copy(list_hbm, list_ref, semaphores.at[3]),
    ]
    for copy in fetched:
        copy.start()
    kept = [
        pltpu.make_async_copy(source_ref, source_hbm, semaphores.at[0]),
        pltpu.make_async_copy(target_ref, target_hbm, semaphores.at[1]),
    ]
    for copy in kept:
        copy.start()

    def prepare_source(tile, _):
        at = at_tile(tile)
        left_ref[at, :] = source_rows(source_ref[:, at].astype(F32))
        return 0

    clear_marks(covered)
    lax.fori_loop(0, source_tiles, prepare_source, 0, unroll=UNROLL)
    for copy in fetched:
        copy.wait()
    highest = highest_of(potential_ref)
    weight[...] = jnp.exp2((potential_ref[...] - highest) * KAPPA)

    def prepare(tile, _):
        at = at_tile(tile)
        cells = target_ref[:, at]
        for piece in range(PIECES):
            right[piece * WIDTH : (piece + 1) * WIDTH, at] = cells
        tail = pieces(squares(cells.astype(F32)) * -GAMMA) + [jnp.ones((PIECES, TILE), F32)]
        tail.append(jnp.zeros((RIGHT - PIECES * WIDTH - 2 * PIECES, TILE), F32))
        right[PIECES * WIDTH : RIGHT, at] = jnp.concatenate(tail, axis=0).astype(BF16)
        share = sums.shape[0] // target_tiles
        sums[pl.ds(pl.multiple_of(tile * share, share), share), :] = jnp.zeros((share, 128), F32)
        return 0

    lax.fori_loop(0, target_tiles, prepare, 0, unroll=UNROLL)

    def step(entry, store, slot):
        alive = (entry < live).astype(jnp.int32)
        source_tile = list_ref[0, entry]
        target_tile = list_ref[1, entry]
        covered[source_tile] = jnp.maximum(covered[source_tile], alive)
        factor = read_line(weight, target_tile) * alive.astype(F32)
        columns = right[:, at_tile(target_tile)]
        for row in range(0, TILE, rows_of):
            at = pl.ds(pl.multiple_of(source_tile * TILE + row, rows_of), rows_of)
            value = jnp.exp2(jnp.dot(left_ref[at, :RIGHT], columns, preferred_element_type=F32))
            stores[store][slot, row : row + rows_of, :] = value.astype(BF16)
            value = value * factor
            sums[at, :] += (value[:, 0:128] + value[:, 128:256]) + (value[:, 256:384] + value[:, 384:512])

    groups(live, step)
    def finish(tile, _):
        terms = jnp.concatenate(pieces(sums[at_tile(tile), :], 2), axis=1).astype(BF16)
        lines = lax.dot_general(jnp.ones((16, 256), BF16), terms, (((1,), (1,)), ((), ())), preferred_element_type=F32)
        write_line(out_ref, tile, jnp.where(covered[tile] > 0, jnp.maximum(lines[0:1], 0.0), ABSENT))
        return 0

    lax.fori_loop(0, source_tiles, finish, 0, unroll=UNROLL)
    smallest = to_potentials(out_ref, highest)
    for copy in kept:
        copy.wait()

    @pl.when(smallest < TRUSTED)
    def _():
        general_lse(
            1, 0, list_ref, live,
            lambda tile: target_ref[:, at_tile(tile)].astype(F32),
            lambda tile: source_ref[:, at_tile(tile)].astype(F32),
            lambda tile: read_line(potential_ref, tile),
            out_ref, top, total,
        )


def column_kernel(
    list_hbm, count_ref, potential_ref, store_0, store_1, store_2, store_3, source_hbm, target_hbm,
    out_ref,
    parts, weight, sums, covered, top, total, source_ref, target_ref, list_ref, semaphore,
):
    stores = (store_0, store_1, store_2, store_3)
    source_tiles = source_ref.shape[1] // TILE
    target_tiles = sums.shape[1] // TILE
    live = count_ref[0, 0]
    fetch = pltpu.make_async_copy(list_hbm, list_ref, semaphore)
    fetch.start()
    highest = highest_of(potential_ref)

    for piece, term in enumerate(pieces(jnp.exp2((potential_ref[...] - highest) * KAPPA))):
        parts[piece] = term

    def prepare(tile, _):
        terms = [read_line(parts.at[piece], tile) for piece in range(PIECES)]
        weight[:, at_tile(tile)] = jnp.concatenate(terms + [jnp.zeros((16 - PIECES, TILE), F32)], axis=0).astype(BF16)
        return 0

    def clear(tile, _):
        sums[:, at_tile(tile)] = jnp.zeros((16, TILE), F32)
        return 0

    clear_marks(covered)
    lax.fori_loop(0, source_tiles, prepare, 0, unroll=UNROLL)
    lax.fori_loop(0, target_tiles, clear, 0, unroll=UNROLL)
    fetch.wait()

    def step(entry, store, slot):
        alive = (entry < live).astype(jnp.int32)
        target_tile = list_ref[1, entry]
        covered[target_tile] = jnp.maximum(covered[target_tile], alive)
        lines = jnp.dot(weight[:, at_tile(list_ref[0, entry])], stores[store][slot], preferred_element_type=F32)
        sums[:, at_tile(target_tile)] += lines * alive.astype(F32)

    groups(live, step)
    def finish(tile, _):
        summed = jnp.sum(sums[:, at_tile(tile)], axis=0, keepdims=True)
        write_line(out_ref, tile, jnp.where(covered[tile] > 0, jnp.maximum(summed, 0.0), ABSENT))
        return 0

    lax.fori_loop(0, target_tiles, finish, 0, unroll=UNROLL)
    smallest = to_potentials(out_ref, highest)

    @pl.when(smallest < TRUSTED)
    def _():
        for hbm, ref in ((source_hbm, source_ref), (target_hbm, target_ref)):
            copy = pltpu.make_async_copy(hbm, ref, semaphore)
            copy.start()
            copy.wait()
        general_lse(
            0, 1, list_ref, live,
            lambda tile: source_ref[:, at_tile(tile)].astype(F32),
            lambda tile: target_ref[:, at_tile(tile)].astype(F32),
            lambda tile: read_line(potential_ref, tile),
            out_ref, top, total,
        )


def row_call(own_list, counts, source_full, target_full, potential):
    source_cells, target_cells = source_full.shape[1], target_full.shape[1]
    slots = own_list.shape[1] // STORES
    return pl.pallas_call(
        row_kernel,
        name="row_sums",
        out_shape=(
            jax.ShapeDtypeStruct((source_cells // 128, 128), F32),
            pltpu.HBM(source_full.shape, BF16),
            pltpu.HBM(target_full.shape, BF16),
        )
        + (pltpu.VMEM((slots, TILE, TILE), BF16),) * STORES,
        in_specs=[HBM, SMEM, VMEM, VMEM, HBM],
        out_specs=(VMEM, HBM, HBM) + (VMEM,) * STORES,
        scratch_shapes=[
            pltpu.VMEM((source_cells, LEFT), BF16),
            pltpu.VMEM((RIGHT, target_cells), BF16),
            pltpu.VMEM((target_cells // 128, 128), F32),
            pltpu.VMEM((source_cells, 128), F32),
            pltpu.SMEM((source_cells // TILE,), jnp.int32),
            pltpu.VMEM((8, source_cells), F32),
            pltpu.VMEM((8, source_cells), F32),
            pltpu.SMEM(own_list.shape, jnp.int32),
            pltpu.VMEM((target_cells // 128, 128), F32),
            pltpu.SemaphoreType.DMA((4,)),
        ],
        compiler_params=pltpu.CompilerParams(vmem_limit_bytes=14 << 20),
    )(in_hbm(own_list), counts, source_full, target_full, in_hbm(potential))


def column_call(own_list, counts, row_potential, stores, source_full, target_full):
    source_cells, target_cells = source_full.shape[1], target_full.shape[1]
    return pl.pallas_call(
        column_kernel,
        name="column_sums",
        out_shape=jax.ShapeDtypeStruct((target_cells // 128, 128), F32),
        in_specs=[HBM, SMEM, VMEM] + [VMEM] * STORES + [HBM, HBM],
        out_specs=VMEM,
        scratch_shapes=[
            pltpu.VMEM((PIECES, source_cells // 128, 128), F32),
            pltpu.VMEM((16, source_cells), BF16),
            pltpu.VMEM((16, target_cells), F32),
            pltpu.SMEM((target_cells // TILE,), jnp.int32),
            pltpu.VMEM((8, target_cells), F32),
            pltpu.VMEM((8, target_cells), F32),
            pltpu.VMEM((WIDTH, source_cells), BF16),
            pltpu.VMEM((WIDTH, target_cells), BF16),
            pltpu.SMEM(own_list.shape, jnp.int32),
            pltpu.SemaphoreType.DMA,
        ],
        compiler_params=pltpu.CompilerParams(vmem_limit_bytes=10 << 20),
    )(in_hbm(own_list), counts, row_potential, *stores, in_hbm(source_full), in_hbm(target_full))


def merged(parts):
    highest = functools.reduce(jnp.maximum, parts)
    summed = sum(jnp.exp((part - highest) * (1.0 / EPSILON)) for part in parts)
    return highest + EPSILON * jnp.log(summed)


def along(axis, size, group, stride, shift):
    pairs = []
    for index in range(size):
        digit = index // stride % group
        pairs.append((index, index + ((digit + shift) % group - digit) * stride))
    return lambda value: lax.ppermute(value, axis, pairs)


def local(source_embed, target_embed, target_potential, log_source_mass, log_target_mass, tile_list, counts):
    over_x = [along("src", 16, 4, 4, shift) for shift in (1, 2, 3)]
    over_z = [along("src", 16, 4, 1, shift) for shift in (1, 2, 3)]
    over_y = [along("tgt", 8, 4, 2, shift) for shift in (1, 2, 3)]
    over_core = along("tgt", 8, 2, 1, 1)

    sources = lax.axis_size("src")
    copies = pl.pallas_call(
        copies_kernel,
        name="target_copies",
        out_shape=pltpu.VMEM((sources,) + target_embed.shape, BF16),
        in_specs=[VMEM],
        out_specs=VMEM,
        compiler_params=pltpu.CompilerParams(vmem_limit_bytes=8 << 20),
    )(target_embed)
    target_full = lax.all_to_all(copies, "src", 0, 0).reshape(WIDTH, -1)
    source_full = lax.all_gather(source_embed, "tgt", axis=0, tiled=True)

    own_list = tile_list[0, 0]

    row, source_kept, target_kept, *stores = row_call(own_list, counts, source_full, target_full, target_potential.reshape(-1, 128))
    row = merged([row, over_core(row)])
    row = merged([row] + [send(row) for send in over_y])
    row_potential = EPSILON * log_source_mass.reshape(-1, 128) - row

    column = column_call(own_list, counts, row_potential, stores, source_kept, target_kept)
    column = merged([column] + [send(column) for send in over_x])
    column = merged([column] + [send(column) for send in over_z])
    column_potential = EPSILON * log_target_mass.reshape(-1, 128) - column
    return row_potential.reshape(-1), column_potential.reshape(-1)


def solution(mesh):
    return jax.shard_map(
        local,
        mesh=mesh,
        in_specs=(
            P("tgt", "src"),
            P("src", "tgt"),
            P("tgt"),
            P("src"),
            P("tgt"),
            P("src", "tgt", None, None),
            P("src", "tgt"),
        ),
        out_specs=(P("src"), P("tgt")),
        check_vma=False,
    )
```

profile of v0, /device:TPU:25, one launch (start us, length us, event | category | flops | bytes accessed | tf_op | source)
XLA Modules:
  0.0 129.9 jit_solution(2046922785363313136)
XLA Ops:
  0.6 0.0 copy-start.1
  0.6 0.8 copy-done.1
  1.5 0.0 copy-start.3
  1.5 1.0 target_copies.1
  2.5 7.6 %all-to-all-start = ((bf16[16,2,16384]{2,1,0:T(2,128)(2,1)}), bf16[16,2,16384]{2,1,0:T(2,128)(2,1)S(1)}, u32[]{:S(2)}, u32[]{:S(2)}) async-start(bf16[16,2,16384]{2,1,0:T(2,128)(2,1)} %target_copies.1), calls=%async_computation | async-start | bytes 2097152 | tf_op jit(solution)/shard_map/all_to_all | solution.py:375
  10.8 14.1 %all-gather = bf16[8,4,8192]{2,1,0:T(4,128)(2,1)S(1)} all-gather(bf16[1,4,8192]{2,1,0:T(4,128)(2,1)} %bitcast.13), channel_id=1, replica_groups=mesh['src'=16,'tgt'=8] {'tgt'}, dimensions={0}, use_global_device_ids=true | all-gather | bytes 589824 | tf_op jit(solution)/shard_map/all_gather | solution.py:376
  24.9 0.1 reshape.27.source_ref
  25.0 0.6 all-to-all-done
  25.6 0.4 reshape.22.target_ref
  26.1 30.8 %row_sums.1 = (f32[64,128]{1,0:T(8,128)S(1)}, bf16[32,8192]{1,0:T(8,128)(2,1)}, bf16[32,16384]{1,0:T(8,128)(2,1)}, bf16[16,512,512]{2,1,0:T(8,128)(2,1)S(1)}, bf...) custom-call(s32[2,64]{1,0:T(2,128)} %bitcast.15, ...), custom_call_target="tpu_custom_call" | custom-call | tf_op jit(solution)/shard_map/row_sums/pallas_call | solution.py:295
  56.9 0.1 collective-permute-start
  57.0 1.2 collective-permute-done
  58.2 0.1 collective-permute-start.3
  58.3 2.0 %collective-permute-start.2 = (f32[64,128]{1,0:T(8,128)S(1)}, f32[64,128]{1,0:T(8,128)S(1)}, u32[]{:S(2)}, u32[]{:S(2)}) collective-permute-start(f32[64,128]{1,0:T(8,128)S(1)} %multiply_add_fusion.1), channel_id=1, source_target_pairs={{0,4},{1,5},{2,6},{3,7},{4,0},{5,1},{6,2},{7,3},{8,12},{9,13},{10,... | collective-permute-start | bytes 98312 | tf_op jit(solution)/shard_map/ppermute | solution.py:357
  60.3 0.6 collective-permute-start.1
  60.9 1.3 collective-permute-done.3
  62.2 0.6 collective-permute-done.2
  62.9 0.6 collective-permute-done.1
  63.5 0.0 copy-done.3
  63.5 0.0 copy-start
  63.5 0.0 copy-start.2
  63.5 5.8 %column_sums.1 = f32[128,128]{1,0:T(8,128)S(1)} custom-call(s32[2,64]{1,0:T(2,128)} %bitcast.16, s32[1,1]{1,0:T(1,128)S(6)} %copy.9.count_ref, f32[64,128]{1,0:T(8,128)S(1)} %bitcast_subtract_fusion.1.potential_ref, bf16[16,512,512]{2,1,0:T(8,128)(2,1)S(1)} %get-tuple-element.10.store_0, bf16[16,512,512]{2,1,0:T(8,128)(2,1)S(1)} %get-tuple-element.11.store_1, ...), custom_call_target="tpu_custom_call" | custom-call | tf_op jit(solution)/shard_map/column_sums/pallas_call | solution.py:324
  69.3 0.0 copy-done
  69.3 10.7 %collective-permute-start.6 = (f32[128,128]{1,0:T(8,128)S(1)}, f32[128,128]{1,0:T(8,128)S(1)}, u32[]{:S(2)}, u32[]{:S(2)}) collective-permute-start(f32[128,128]{1,0:T(8,128)S(1)} %column_sums.1), channel_id=1, source_target_pairs={{0,96},{8,104},{16,112},{24,120},{32,0},{40,8},{48,16},{56,24},{64... | collective-permute-start | bytes 196616 | tf_op jit(solution)/shard_map/ppermute | solution.py:357
  80.1 4.4 %collective-permute-start.5 = (f32[128,128]{1,0:T(8,128)S(1)}, f32[128,128]{1,0:T(8,128)S(1)}, u32[]{:S(2)}, u32[]{:S(2)}) collective-permute-start(f32[128,128]{1,0:T(8,128)S(1)} %column_sums.1), channel_id=1, source_target_pairs={{0,64},{8,72},{16,80},{24,88},{32,96},{40,104},{48,112},{56,120},{... | collective-permute-start | bytes 196616 | tf_op jit(solution)/shard_map/ppermute | solution.py:357
  84.5 0.8 collective-permute-start.4
  85.2 0.0 collective-permute-done.6
  85.3 0.9 collective-permute-done.5
  86.1 2.7 %collective-permute-done.4 = f32[128,128]{1,0:T(8,128)S(1)} collective-permute-done((f32[128,128]{1,0:T(8,128)S(1)}, f32[128,128]{1,0:T(8,128)S(1)}, u32[]{:S(2)}, u32[]{:S(2)}) %collective-permute-start.4) | collective-permute-done | bytes 65568 | tf_op jit(solution)/shard_map/ppermute | solution.py:357
  88.8 0.1 multiply_add_fusion
  88.9 0.1 collective-permute-start.9
  89.0 35.9 %collective-permute-start.8 = (f32[128,128]{1,0:T(8,128)S(1)}, f32[128,128]{1,0:T(8,128)S(1)}, u32[]{:S(2)}, u32[]{:S(2)}) collective-permute-start(f32[128,128]{1,0:T(8,128)S(1)} %multiply_add_fusion), channel_id=1, source_target_pairs={{0,16},{8,24},{16,0},{24,8},{32,48},{40,56},{48,32},{56,40},{64,80... | collective-permute-start | bytes 196616 | tf_op jit(solution)/shard_map/ppermute | solution.py:357
  124.9 0.8 collective-permute-start.7
  125.6 0.0 collective-permute-done.9
  125.6 0.9 collective-permute-done.8
  126.5 2.7 %collective-permute-done.7 = f32[128,128]{1,0:T(8,128)S(1)} collective-permute-done((f32[128,128]{1,0:T(8,128)S(1)}, f32[128,128]{1,0:T(8,128)S(1)}, u32[]{:S(2)}, u32[]{:S(2)}) %collective-permute-start.7) | collective-permute-done | bytes 65568 | tf_op jit(solution)/shard_map/ppermute | solution.py:357
  129.2 0.0 copy-done.2
  129.2 0.7 fusion
  (2 shorter events, 0.1 us)
Async XLA Ops:
  0.6 0.8 copy-start.1
  1.5 62.0 %copy-start.3 = (f32[8192]{0:T(1024)S(1)}, f32[8192]{0:T(1024)}, u32[]{:S(2)}) copy-start(f32[8192]{0:T(1024)} %param.10) | copy-start | bytes 98308
  2.5 23.1 %all-to-all-start = ((bf16[16,2,16384]{2,1,0:T(2,128)(2,1)}), bf16[16,2,16384]{2,1,0:T(2,128)(2,1)S(1)}, u32[]{:S(2)}, u32[]{:S(2)}) async-start(bf16[16,2,16384]{2,1,0:T(2,128)(2,1)} %target_copies.1), calls=%async_computation | async-start | bytes 2097152 | tf_op jit(solution)/shard_map/all_to_all | solution.py:375
  56.9 1.3 collective-permute-start
  58.2 4.0 %collective-permute-start.3 = (f32[64,128]{1,0:T(8,128)S(1)}, f32[64,128]{1,0:T(8,128)S(1)}, u32[]{:S(2)}, u32[]{:S(2)}) collective-permute-start(f32[64,128]{1,0:T(8,128)S(1)} %multiply_add_fusion.1), channel_id=1, source_target_pairs={{0,6},{1,7},{2,0},{3,1},{4,2},{5,3},{6,4},{7,5},{8,14},{9,15},{10,... | collective-permute-start | bytes 98312 | tf_op jit(solution)/shard_map/ppermute | solution.py:357
  58.3 4.6 %collective-permute-start.2 = (f32[64,128]{1,0:T(8,128)S(1)}, f32[64,128]{1,0:T(8,128)S(1)}, u32[]{:S(2)}, u32[]{:S(2)}) collective-permute-start(f32[64,128]{1,0:T(8,128)S(1)} %multiply_add_fusion.1), channel_id=1, source_target_pairs={{0,4},{1,5},{2,6},{3,7},{4,0},{5,1},{6,2},{7,3},{8,12},{9,13},{10,... | collective-permute-start | bytes 98312 | tf_op jit(solution)/shard_map/ppermute | solution.py:357
  60.3 3.2 %collective-permute-start.1 = (f32[64,128]{1,0:T(8,128)S(1)}, f32[64,128]{1,0:T(8,128)S(1)}, u32[]{:S(2)}, u32[]{:S(2)}) collective-permute-start(f32[64,128]{1,0:T(8,128)S(1)} %multiply_add_fusion.1), channel_id=1, source_target_pairs={{0,2},{1,3},{2,4},{3,5},{4,6},{5,7},{6,0},{7,1},{8,10},{9,11},{10,... | collective-permute-start | bytes 98312 | tf_op jit(solution)/shard_map/ppermute | solution.py:357
  63.5 5.8 %copy-start = (f32[64,128]{1,0:T(8,128)}, f32[64,128]{1,0:T(8,128)S(1)}, u32[]{:S(2)}) copy-start(f32[64,128]{1,0:T(8,128)S(1)} %bitcast_subtract_fusion.1.potential_ref) | copy-start | bytes 98308
  63.5 65.6 %copy-start.2 = (f32[16384]{0:T(1024)S(1)}, f32[16384]{0:T(1024)}, u32[]{:S(2)}) copy-start(f32[16384]{0:T(1024)} %param.11) | copy-start | bytes 196612
  69.3 15.9 %collective-permute-start.6 = (f32[128,128]{1,0:T(8,128)S(1)}, f32[128,128]{1,0:T(8,128)S(1)}, u32[]{:S(2)}, u32[]{:S(2)}) collective-permute-start(f32[128,128]{1,0:T(8,128)S(1)} %column_sums.1), channel_id=1, source_target_pairs={{0,96},{8,104},{16,112},{24,120},{32,0},{40,8},{48,16},{56,24},{64... | collective-permute-start | bytes 196616 | tf_op jit(solution)/shard_map/ppermute | solution.py:357
  80.1 6.1 %collective-permute-start.5 = (f32[128,128]{1,0:T(8,128)S(1)}, f32[128,128]{1,0:T(8,128)S(1)}, u32[]{:S(2)}, u32[]{:S(2)}) collective-permute-start(f32[128,128]{1,0:T(8,128)S(1)} %column_sums.1), channel_id=1, source_target_pairs={{0,64},{8,72},{16,80},{24,88},{32,96},{40,104},{48,112},{56,120},{... | collective-permute-start | bytes 196616 | tf_op jit(solution)/shard_map/ppermute | solution.py:357
  84.5 4.3 %collective-permute-start.4 = (f32[128,128]{1,0:T(8,128)S(1)}, f32[128,128]{1,0:T(8,128)S(1)}, u32[]{:S(2)}, u32[]{:S(2)}) collective-permute-start(f32[128,128]{1,0:T(8,128)S(1)} %column_sums.1), channel_id=1, source_target_pairs={{0,32},{8,40},{16,48},{24,56},{32,64},{40,72},{48,80},{56,88},{64,... | collective-permute-start | bytes 196616 | tf_op jit(solution)/shard_map/ppermute | solution.py:357
  88.9 36.7 %collective-permute-start.9 = (f32[128,128]{1,0:T(8,128)S(1)}, f32[128,128]{1,0:T(8,128)S(1)}, u32[]{:S(2)}, u32[]{:S(2)}) collective-permute-start(f32[128,128]{1,0:T(8,128)S(1)} %multiply_add_fusion), channel_id=1, source_target_pairs={{0,24},{8,0},{16,8},{24,16},{32,56},{40,32},{48,40},{56,48},{64,88... | collective-permute-start | bytes 196616 | tf_op jit(solution)/shard_map/ppermute | solution.py:357
  89.0 37.5 %collective-permute-start.8 = (f32[128,128]{1,0:T(8,128)S(1)}, f32[128,128]{1,0:T(8,128)S(1)}, u32[]{:S(2)}, u32[]{:S(2)}) collective-permute-start(f32[128,128]{1,0:T(8,128)S(1)} %multiply_add_fusion), channel_id=1, source_target_pairs={{0,16},{8,24},{16,0},{24,8},{32,48},{40,56},{48,32},{56,40},{64,80... | collective-permute-start | bytes 196616 | tf_op jit(solution)/shard_map/ppermute | solution.py:357
  124.9 4.3 %collective-permute-start.7 = (f32[128,128]{1,0:T(8,128)S(1)}, f32[128,128]{1,0:T(8,128)S(1)}, u32[]{:S(2)}, u32[]{:S(2)}) collective-permute-start(f32[128,128]{1,0:T(8,128)S(1)} %multiply_add_fusion), channel_id=1, source_target_pairs={{0,8},{8,16},{16,24},{24,0},{32,40},{40,48},{48,56},{56,32},{64,72... | collective-permute-start | bytes 196616 | tf_op jit(solution)/shard_map/ppermute | solution.py:357
where the time goes:
time: 132 us; the launch traced here: 130 us
  starting transfers between devices  63.1 us (48%)
  Pallas kernels  37.6 us (28%)
  blocking collectives  14.1 us (11%)
  waiting for transfers between devices  11.4 us (9%)
  between operations  1.39 us (1%)
  local copies, waits for them, and re-layouts  1.38 us (1%)
    ppermute x10, starting transfers between devices, along(): return lambda value: lax.ppermute(value, axis, pairs)  55.5 us
    pallas_call x1, Pallas kernels, row_call(): pl.pallas_call(row_kernel, name='row_sums', out_shape=(jax.ShapeDtypeStru...  30.8 us
    all_gather x1, blocking collectives, local(): source_full = lax.all_gather(source_embed, 'tgt', axis=0, tiled=True)  14.1 us
    ppermute x10, waiting for transfers between devices, along(): return lambda value: lax.ppermute(value, axis, pairs)  10.8 us
    all_to_all x1, starting transfers between devices, local(): target_full = lax.all_to_all(copies, 'src', 0, 0).reshape(WIDTH, -1)  7.6 us
    pallas_call x1, Pallas kernels, column_call(): pl.pallas_call(column_kernel, name='column_sums', out_shape=jax.ShapeDtyp...  5.76 us
  transfers between devices with their start and end apart: 11, of which 9 were waited for; matrix products, arithmetic and copies ran while one was open for 0% of the time, Pallas kernels for 0%

commit v1 on v0

--- a/solution.py
+++ b/solution.py
@@ -14,7 +14,7 @@
 LEFT = 128
 RIGHT = 112
 DEPTH = 48
-TOGETHER = 32
+TOGETHER = 16
 UNROLL = 8
 STORES = 4
 EPSILON = 0.1

time: 132 us -> 137 us (1.038)
  the two profiles are of different devices: /device:TPU:25 before, /device:TPU:8 now
where the time goes in v1:
time: 137 us; the launch traced here: 136 us
  starting transfers between devices  79.1 us (58%)
  Pallas kernels  21 us (15%)
  waiting for transfers between devices  19.2 us (14%)
  blocking collectives  13.5 us (10%)
  local copies, waits for them, and re-layouts  1.38 us (1%)
  between operations  1.37 us (1%)
    ppermute x10, starting transfers between devices, along(): return lambda value: lax.ppermute(value, axis, pairs)  71.2 us
    ppermute x10, waiting for transfers between devices, along(): return lambda value: lax.ppermute(value, axis, pairs)  15.8 us
    all_gather x1, blocking collectives, local(): source_full = lax.all_gather(source_embed, 'tgt', axis=0, tiled=True)  13.5 us
    pallas_call x1, Pallas kernels, row_call(): pl.pallas_call(row_kernel, name='row_sums', out_shape=(jax.ShapeDtypeStru...  10.1 us
    pallas_call x1, Pallas kernels, column_call(): pl.pallas_call(column_kernel, name='column_sums', out_shape=jax.ShapeDtyp...  9.83 us
    all_to_all x1, starting transfers between devices, local(): target_full = lax.all_to_all(copies, 'src', 0, 0).reshape(WIDTH, -1)  7.88 us
    all_to_all x1, waiting for transfers between devices, local(): target_full = lax.all_to_all(copies, 'src', 0, 0).reshape(WIDTH, -1)  3.37 us
  transfers between devices with their start and end apart: 11, of which 11 were waited for; matrix products, arithmetic and copies ran while one was open for 0% of the time, Pallas kernels for 0%

profile of v1, /device:TPU:8, one launch (start us, length us, event | category | flops | bytes accessed | tf_op | source)
XLA Modules:
  0.0 136.4 jit_solution(17422007413612739903)
XLA Ops:
  0.6 0.0 copy-start.1
  0.6 0.8 copy-done.1
  1.5 0.0 copy-start.3
  1.5 1.0 target_copies.1
  2.5 7.9 %all-to-all-start = ((bf16[16,2,16384]{2,1,0:T(2,128)(2,1)}), bf16[16,2,16384]{2,1,0:T(2,128)(2,1)S(1)}, u32[]{:S(2)}, u32[]{:S(2)}) async-start(bf16[16,2,16384]{2,1,0:T(2,128)(2,1)} %target_copies.1), calls=%async_computation | async-start | bytes 2097152 | tf_op jit(solution)/shard_map/all_to_all | solution.py:375
  11.1 13.5 %all-gather = bf16[8,4,8192]{2,1,0:T(4,128)(2,1)S(1)} all-gather(bf16[1,4,8192]{2,1,0:T(4,128)(2,1)} %bitcast.13), channel_id=1, replica_groups=mesh['src'=16,'tgt'=8] {'tgt'}, dimensions={0}, use_global_device_ids=true | all-gather | bytes 589824 | tf_op jit(solution)/shard_map/all_gather | solution.py:376
  24.6 0.1 reshape.27.source_ref
  24.7 3.4 %all-to-all-done = bf16[16,2,16384]{2,1,0:T(2,128)(2,1)S(1)} async-done(((bf16[16,2,16384]{2,1,0:T(2,128)(2,1)}), bf16[16,2,16384]{2,1,0:T(2,128)(2,1)S(1)}, u32[]{:S(2)}, u32[]{:S(2)}) %all-to-all-start) | async-done | bytes 1048608 | tf_op jit(solution)/shard_map/all_to_all | solution.py:375
  28.1 0.4 reshape.22.target_ref
  28.5 10.1 %row_sums.1 = (f32[64,128]{1,0:T(8,128)S(1)}, bf16[32,8192]{1,0:T(8,128)(2,1)}, bf16[32,16384]{1,0:T(8,128)(2,1)}, bf16[16,512,512]{2,1,0:T(8,128)(2,1)S(1)}, bf...) custom-call(s32[2,64]{1,0:T(2,128)} %bitcast.15, ...), custom_call_target="tpu_custom_call" | custom-call | tf_op jit(solution)/shard_map/row_sums/pallas_call | solution.py:295
  38.7 0.1 collective-permute-start
  38.7 1.2 collective-permute-done
  40.0 0.5 collective-permute-start.3
  40.5 33.3 %collective-permute-start.2 = (f32[64,128]{1,0:T(8,128)S(1)}, f32[64,128]{1,0:T(8,128)S(1)}, u32[]{:S(2)}, u32[]{:S(2)}) collective-permute-start(f32[64,128]{1,0:T(8,128)S(1)} %multiply_add_fusion.1), channel_id=1, source_target_pairs={{0,4},{1,5},{2,6},{3,7},{4,0},{5,1},{6,2},{7,3},{8,12},{9,13},{10,... | collective-permute-start | bytes 98312 | tf_op jit(solution)/shard_map/ppermute | solution.py:357
  73.8 0.0 collective-permute-start.1
  73.8 0.4 collective-permute-done.3
  74.2 1.9 %collective-permute-done.2 = f32[64,128]{1,0:T(8,128)S(1)} collective-permute-done((f32[64,128]{1,0:T(8,128)S(1)}, f32[64,128]{1,0:T(8,128)S(1)}, u32[]{:S(2)}, u32[]{:S(2)}) %collective-permute-start.2) | collective-permute-done | bytes 32800 | tf_op jit(solution)/shard_map/ppermute | solution.py:357
  76.1 1.6 %collective-permute-done.1 = f32[64,128]{1,0:T(8,128)S(1)} collective-permute-done((f32[64,128]{1,0:T(8,128)S(1)}, f32[64,128]{1,0:T(8,128)S(1)}, u32[]{:S(2)}, u32[]{:S(2)}) %collective-permute-start.1) | collective-permute-done | bytes 32800 | tf_op jit(solution)/shard_map/ppermute | solution.py:357
  77.7 0.0 copy-done.3
  77.8 0.0 copy-start
  77.8 0.0 copy-start.2
  77.8 9.8 %column_sums.1 = f32[128,128]{1,0:T(8,128)S(1)} custom-call(s32[2,64]{1,0:T(2,128)} %bitcast.16, s32[1,1]{1,0:T(1,128)S(6)} %copy.9.count_ref, f32[64,128]{1,0:T(8,128)S(1)} %bitcast_subtract_fusion.1.potential_ref, bf16[16,512,512]{2,1,0:T(8,128)(2,1)S(1)} %get-tuple-element.10.store_0, bf16[16,512,512]{2,1,0:T(8,128)(2,1)S(1)} %get-tuple-element.11.store_1, ...), custom_call_target="tpu_custom_call" | custom-call | tf_op jit(solution)/shard_map/column_sums/pallas_call | solution.py:324
  87.6 0.0 copy-done
  87.6 5.9 %collective-permute-start.6 = (f32[128,128]{1,0:T(8,128)S(1)}, f32[128,128]{1,0:T(8,128)S(1)}, u32[]{:S(2)}, u32[]{:S(2)}) collective-permute-start(f32[128,128]{1,0:T(8,128)S(1)} %column_sums.1), channel_id=1, source_target_pairs={{0,96},{8,104},{16,112},{24,120},{32,0},{40,8},{48,16},{56,24},{64... | collective-permute-start | bytes 196616 | tf_op jit(solution)/shard_map/ppermute | solution.py:357
  93.5 0.0 collective-permute-start.5
  93.6 0.9 collective-permute-start.4
  94.5 1.6 %collective-permute-done.6 = f32[128,128]{1,0:T(8,128)S(1)} collective-permute-done((f32[128,128]{1,0:T(8,128)S(1)}, f32[128,128]{1,0:T(8,128)S(1)}, u32[]{:S(2)}, u32[]{:S(2)}) %collective-permute-start.6) | collective-permute-done | bytes 65568 | tf_op jit(solution)/shard_map/ppermute | solution.py:357
  96.1 3.4 %collective-permute-done.5 = f32[128,128]{1,0:T(8,128)S(1)} collective-permute-done((f32[128,128]{1,0:T(8,128)S(1)}, f32[128,128]{1,0:T(8,128)S(1)}, u32[]{:S(2)}, u32[]{:S(2)}) %collective-permute-start.5) | collective-permute-done | bytes 65568 | tf_op jit(solution)/shard_map/ppermute | solution.py:357
  99.4 0.3 collective-permute-done.4
  99.7 0.1 multiply_add_fusion
  99.8 3.2 %collective-permute-start.9 = (f32[128,128]{1,0:T(8,128)S(1)}, f32[128,128]{1,0:T(8,128)S(1)}, u32[]{:S(2)}, u32[]{:S(2)}) collective-permute-start(f32[128,128]{1,0:T(8,128)S(1)} %multiply_add_fusion), channel_id=1, source_target_pairs={{0,24},{8,0},{16,8},{24,16},{32,56},{40,32},{48,40},{56,48},{64,88... | collective-permute-start | bytes 196616 | tf_op jit(solution)/shard_map/ppermute | solution.py:357
  103.0 27.2 %collective-permute-start.8 = (f32[128,128]{1,0:T(8,128)S(1)}, f32[128,128]{1,0:T(8,128)S(1)}, u32[]{:S(2)}, u32[]{:S(2)}) collective-permute-start(f32[128,128]{1,0:T(8,128)S(1)} %multiply_add_fusion), channel_id=1, source_target_pairs={{0,16},{8,24},{16,0},{24,8},{32,48},{40,56},{48,32},{56,40},{64,80... | collective-permute-start | bytes 196616 | tf_op jit(solution)/shard_map/ppermute | solution.py:357
  130.2 0.0 collective-permute-start.7
  130.2 0.2 collective-permute-done.9
  130.4 2.1 %collective-permute-done.8 = f32[128,128]{1,0:T(8,128)S(1)} collective-permute-done((f32[128,128]{1,0:T(8,128)S(1)}, f32[128,128]{1,0:T(8,128)S(1)}, u32[]{:S(2)}, u32[]{:S(2)}) %collective-permute-start.8) | collective-permute-done | bytes 65568 | tf_op jit(solution)/shard_map/ppermute | solution.py:357
  132.5 3.2 %collective-permute-done.7 = f32[128,128]{1,0:T(8,128)S(1)} collective-permute-done((f32[128,128]{1,0:T(8,128)S(1)}, f32[128,128]{1,0:T(8,128)S(1)}, u32[]{:S(2)}, u32[]{:S(2)}) %collective-permute-start.7) | collective-permute-done | bytes 65568 | tf_op jit(solution)/shard_map/ppermute | solution.py:357
  135.7 0.0 copy-done.2
  135.7 0.7 fusion
  (2 shorter events, 0.1 us)
Async XLA Ops:
  0.6 0.8 copy-start.1
  1.5 76.2 %copy-start.3 = (f32[8192]{0:T(1024)S(1)}, f32[8192]{0:T(1024)}, u32[]{:S(2)}) copy-start(f32[8192]{0:T(1024)} %param.10) | copy-start | bytes 98308
  2.5 25.6 %all-to-all-start = ((bf16[16,2,16384]{2,1,0:T(2,128)(2,1)}), bf16[16,2,16384]{2,1,0:T(2,128)(2,1)S(1)}, u32[]{:S(2)}, u32[]{:S(2)}) async-start(bf16[16,2,16384]{2,1,0:T(2,128)(2,1)} %target_copies.1), calls=%async_computation | async-start | bytes 2097152 | tf_op jit(solution)/shard_map/all_to_all | solution.py:375
  38.7 1.3 collective-permute-start
  40.0 34.3 %collective-permute-start.3 = (f32[64,128]{1,0:T(8,128)S(1)}, f32[64,128]{1,0:T(8,128)S(1)}, u32[]{:S(2)}, u32[]{:S(2)}) collective-permute-start(f32[64,128]{1,0:T(8,128)S(1)} %multiply_add_fusion.1), channel_id=1, source_target_pairs={{0,6},{1,7},{2,0},{3,1},{4,2},{5,3},{6,4},{7,5},{8,14},{9,15},{10,... | collective-permute-start | bytes 98312 | tf_op jit(solution)/shard_map/ppermute | solution.py:357
  40.5 35.6 %collective-permute-start.2 = (f32[64,128]{1,0:T(8,128)S(1)}, f32[64,128]{1,0:T(8,128)S(1)}, u32[]{:S(2)}, u32[]{:S(2)}) collective-permute-start(f32[64,128]{1,0:T(8,128)S(1)} %multiply_add_fusion.1), channel_id=1, source_target_pairs={{0,4},{1,5},{2,6},{3,7},{4,0},{5,1},{6,2},{7,3},{8,12},{9,13},{10,... | collective-permute-start | bytes 98312 | tf_op jit(solution)/shard_map/ppermute | solution.py:357
  73.8 3.9 %collective-permute-start.1 = (f32[64,128]{1,0:T(8,128)S(1)}, f32[64,128]{1,0:T(8,128)S(1)}, u32[]{:S(2)}, u32[]{:S(2)}) collective-permute-start(f32[64,128]{1,0:T(8,128)S(1)} %multiply_add_fusion.1), channel_id=1, source_target_pairs={{0,2},{1,3},{2,4},{3,5},{4,6},{5,7},{6,0},{7,1},{8,10},{9,11},{10,... | collective-permute-start | bytes 98312 | tf_op jit(solution)/shard_map/ppermute | solution.py:357
  77.8 9.9 %copy-start = (f32[64,128]{1,0:T(8,128)}, f32[64,128]{1,0:T(8,128)S(1)}, u32[]{:S(2)}) copy-start(f32[64,128]{1,0:T(8,128)S(1)} %bitcast_subtract_fusion.1.potential_ref) | copy-start | bytes 98308
  77.8 57.9 %copy-start.2 = (f32[16384]{0:T(1024)S(1)}, f32[16384]{0:T(1024)}, u32[]{:S(2)}) copy-start(f32[16384]{0:T(1024)} %param.11) | copy-start | bytes 196612
  87.6 8.4 %collective-permute-start.6 = (f32[128,128]{1,0:T(8,128)S(1)}, f32[128,128]{1,0:T(8,128)S(1)}, u32[]{:S(2)}, u32[]{:S(2)}) collective-permute-start(f32[128,128]{1,0:T(8,128)S(1)} %column_sums.1), channel_id=1, source_target_pairs={{0,96},{8,104},{16,112},{24,120},{32,0},{40,8},{48,16},{56,24},{64... | collective-permute-start | bytes 196616 | tf_op jit(solution)/shard_map/ppermute | solution.py:357
  93.5 5.9 %collective-permute-start.5 = (f32[128,128]{1,0:T(8,128)S(1)}, f32[128,128]{1,0:T(8,128)S(1)}, u32[]{:S(2)}, u32[]{:S(2)}) collective-permute-start(f32[128,128]{1,0:T(8,128)S(1)} %column_sums.1), channel_id=1, source_target_pairs={{0,64},{8,72},{16,80},{24,88},{32,96},{40,104},{48,112},{56,120},{... | collective-permute-start | bytes 196616 | tf_op jit(solution)/shard_map/ppermute | solution.py:357
  93.6 6.2 %collective-permute-start.4 = (f32[128,128]{1,0:T(8,128)S(1)}, f32[128,128]{1,0:T(8,128)S(1)}, u32[]{:S(2)}, u32[]{:S(2)}) collective-permute-start(f32[128,128]{1,0:T(8,128)S(1)} %column_sums.1), channel_id=1, source_target_pairs={{0,32},{8,40},{16,48},{24,56},{32,64},{40,72},{48,80},{56,88},{64,... | collective-permute-start | bytes 196616 | tf_op jit(solution)/shard_map/ppermute | solution.py:357
  99.8 30.6 %collective-permute-start.9 = (f32[128,128]{1,0:T(8,128)S(1)}, f32[128,128]{1,0:T(8,128)S(1)}, u32[]{:S(2)}, u32[]{:S(2)}) collective-permute-start(f32[128,128]{1,0:T(8,128)S(1)} %multiply_add_fusion), channel_id=1, source_target_pairs={{0,24},{8,0},{16,8},{24,16},{32,56},{40,32},{48,40},{56,48},{64,88... | collective-permute-start | bytes 196616 | tf_op jit(solution)/shard_map/ppermute | solution.py:357
  103.0 29.5 %collective-permute-start.8 = (f32[128,128]{1,0:T(8,128)S(1)}, f32[128,128]{1,0:T(8,128)S(1)}, u32[]{:S(2)}, u32[]{:S(2)}) collective-permute-start(f32[128,128]{1,0:T(8,128)S(1)} %multiply_add_fusion), channel_id=1, source_target_pairs={{0,16},{8,24},{16,0},{24,8},{32,48},{40,56},{48,32},{56,40},{64,80... | collective-permute-start | bytes 196616 | tf_op jit(solution)/shard_map/ppermute | solution.py:357
  130.2 5.5 %collective-permute-start.7 = (f32[128,128]{1,0:T(8,128)S(1)}, f32[128,128]{1,0:T(8,128)S(1)}, u32[]{:S(2)}, u32[]{:S(2)}) collective-permute-start(f32[128,128]{1,0:T(8,128)S(1)} %multiply_add_fusion), channel_id=1, source_target_pairs={{0,8},{8,16},{16,24},{24,0},{32,40},{40,48},{48,56},{56,32},{64,72... | collective-permute-start | bytes 196616 | tf_op jit(solution)/shard_map/ppermute | solution.py:357
